TPU v7x, 32 devices: a whole 2x2x4 slice. The times are simulated.
32 devices in a mesh: groups: 2 (over y), block: 4 (over z), term: 2 (over x), half: 2 (over core).
Axes of the slice: x: 2, y: 2, z: 4, core: 2. Of those that a mesh axis runs over, the one named last changes fastest.
Arguments:
- psi_blocks: bfloat16 [256, 256, 256], P(('groups', 'block'), 'half'), parts along dimension 0, may hold values from -6 to 6
- left_env: bfloat16 [16, 4, 256, 256], P(('groups', 'term'), 'block', 'half'), parts along dimension 0, may hold values from -0.375 to 0.375
- right_env: bfloat16 [16, 4, 256, 256], P(('groups', 'term'), 'block'), parts along dimension 0, may hold values from -0.375 to 0.375
- right_owner: int32 [256, 1], P('groups'), parts along dimension 0, may hold values from 0 to 3; in each aligned block of 32 rows (0 to 31, 32 to 63, ...) at most 16 rows name the same one
Outputs:
- hpsi: bfloat16 [512, 256, 256], P(('groups', 'block', 'term'), 'half'), parts along dimension 0
There are 2 independent parts, one for each index of `groups`. A program takes and returns all parts, laid end to end along the dimension named above; each array names one. Nothing has to cross between parts.
Inputs may be any that keep to these rules, and one draw needn't show every extreme that they name: `right_owner`: among the 32 blocks of one left sector at most 16 have the same right sector, and in every draw some left sector has exactly 16 blocks with one right sector; every right sector occurs.
All inputs are finite; a program needn't handle non-finite values.
Results may differ from a plain program's by a relative error of at most 0.0059.
Values may be sent and summed in bfloat16 or wider, within the bound.
A program may use at most 128 MiB of HBM per device.

v0:
```python
import jax
import jax.numpy as jnp
from jax import lax
from jax.sharding import PartitionSpec as P


def shards(psi_blocks, left_env, right_env, right_owner):
    n_block = lax.axis_size("block")
    source = lax.axis_index("block")
    per_sector = psi_blocks.shape[0]
    capacity = max(2, 2 * per_sector // n_block)
    rows_half = psi_blocks.shape[1]
    block_width = psi_blocks.shape[2]
    terms_here = left_env.shape[0]
    own_targets = lax.dynamic_slice_in_dim(right_owner[:, 0], source * per_sector, per_sector)
    matches = (own_targets[:, None] == own_targets[None, :]).astype(jnp.int32)
    position = jnp.arange(per_sector, dtype=jnp.int32)
    earlier_mask = (position[None, :] < position[:, None]).astype(jnp.int32)
    ranking = jnp.sum(matches * earlier_mask, axis=1)
    slot_target = own_targets * capacity + ranking
    dispatch = (
        slot_target[:, None] == jnp.arange(n_block * capacity, dtype=jnp.int32)[None, :]
    ).astype(jnp.bfloat16)
    left_rows = left_env[:, 0]
    blended = jnp.einsum(
        "wik,bkc->wbic",
        left_rows,
        lax.all_gather(psi_blocks, "half", axis=1, tiled=True),
        preferred_element_type=jnp.float32,
    ).astype(jnp.bfloat16)
    outgoing = jnp.einsum(
        "bs,wbrc->wsrc", dispatch, blended, preferred_element_type=jnp.float32
    ).astype(jnp.bfloat16)
    outgoing = outgoing.reshape(terms_here, n_block, capacity, rows_half, block_width)
    arrived = lax.all_to_all(outgoing, "block", split_axis=1, concat_axis=1, tiled=True)
    arrived = arrived.reshape(terms_here, n_block * capacity, rows_half, block_width)
    partial_value = jnp.zeros((n_block * capacity, rows_half, block_width), jnp.float32)
    for term_index in range(terms_here):
        partial_value = partial_value + jnp.einsum(
            "src,cn->srn",
            arrived[term_index],
            right_env[term_index, 0],
            preferred_element_type=jnp.float32,
        )
    return lax.psum_scatter(
        partial_value.astype(jnp.bfloat16), "term", scatter_dimension=0, tiled=True
    )


def solution(mesh):
    in_specs = (
        P(("groups", "block"), "half", None),
        P(("groups", "term"), "block", "half", None),
        P(("groups", "term"), "block", None, None),
        P("groups", None),
    )
    out_specs = P(("groups", "block", "term"), "half", None)
    return jax.shard_map(shards, mesh=mesh, in_specs=in_specs, out_specs=out_specs, check_vma=False)
```

profile of v0, /device:TPU:0, one launch (start us, length us, event | category | flops | bytes accessed | tf_op | source)
XLA Modules:
  0.0 533.1 jit_solution(7700718943217263475)
XLA Ops:
  6.5 0.0 copy-start
  6.5 0.0 copy-start.6
  6.5 0.0 all-gather.2.cloned.1.call-start
  6.5 4.1 copy.14
  10.7 0.0 all-gather.2.cloned.1.call-update
  10.7 0.0 reduce-scatter.2.cloned.1.call-start
  10.7 0.0 copy-done.6
  10.7 0.1 fusion.17
  10.8 0.2 select_reduce_fusion
  11.0 0.1 fusion.16
  11.1 15.4 %all-gather.2.cloned.1.call-done = bf16[32,256,256]{1,2,0:T(8,128)(2,1)} async-done(((bf16[32,128,256]{1,2,0:T(8,128)(2,1)}), bf16[32,256,256]{1,2,0:T(8,128)(2,1)}) %all-gather.2.cloned.1.call-update) | async-done | bytes 4194320 | tf_op jit(solution)/shard_map/all_gather | solution.py:28
  26.5 0.0 copy-done
  26.5 6.7 %convert_bitcast_fusion = bf16[4,32,128,256]{2,3,0,1:T(8,128)(2,1)} fusion(bf16[32,256,256]{1,2,0:T(8,128)(2,1)} %all-gather.2.cloned.1.call-done, bf16[4,1,128,256]{3,2,1,0:T(8,128)(2,1)S(1)} %copy-done), kind=kOutput, calls=%fused_computation.2 | convolution fusion | flops 2151677952 | bytes 12845056 | tf_op jit(solution)/shard_map/wik,bkc->wbic/dot_general | solution.py:25
  33.2 14.6 %copy.15 = bf16[4,32,128,256]{3,1,2,0:T(8,128)(2,1)} copy(bf16[4,32,128,256]{2,3,0,1:T(8,128)(2,1)} %convert_bitcast_fusion) | data formatting | bytes 16777216 | tf_op jit(solution)/shard_map/convert_element_type | solution.py:30
  47.9 13.7 %convolution_convert_fusion = bf16[4,128,256,64]{2,3,1,0:T(8,128)(2,1)} fusion(bf16[4,32,128,256]{3,1,2,0:T(8,128)(2,1)} %copy.15, s32[32]{0:T(128)S(1)} %fusion.16), kind=kOutput, calls=%fused_computation | convolution fusion | flops 545261568 | bytes 25165952 | tf_op jit(solution)/shard_map/bs,wbrc->wsrc/dot_general | solution.py:31
  61.6 8.2 %copy.16 = bf16[4,4,16,128,256]{4,2,3,0,1:T(8,128)(2,1)S(1)} copy(bf16[4,4,16,128,256]{4,2,1,3,0:T(8,128)(2,1)} %bitcast.56) | data formatting | bytes 33554432 | tf_op jit(solution)/shard_map/reshape | solution.py:34
  69.8 367.9 %all_to_all.5 = bf16[4,4,16,128,256]{4,2,3,0,1:T(8,128)(2,1)S(1)} all-to-all(bf16[4,4,16,128,256]{4,2,3,0,1:T(8,128)(2,1)S(1)} %copy.16), channel_id=1, replica_groups=mesh['groups'=2,'block'=4,'term'=2,'half'=2] {'block'}, dimensions={1} | all-to-all | bytes 33554432 | tf_op jit(solution)/shard_map/all_to_all | solution.py:35
  437.7 6.0 %fusion.18 = (bf16[1,4,16,128,256]{4,2,3,0,1:T(8,128)(2,1)}, bf16[1,4,16,128,256]{4,2,3,0,1:T(8,128)(2,1)}, bf16[1,4,16,128,256]{4,2,3,0,1:T(8,128)(2,1)}, bf16[1,4,16,128,256]{4,2,3,0,1:T(8,128)(2,1)}) fusion(bf16[4,4,16,128,256]{4,2,3,0,1:T(8,128)(2,1)S(1)} %all_to_all.5), kind=kLoop, calls=%fused_computation.25 | loop fusion | bytes 33554432 | tf_op jit(solution)/shard_map/slice | solution.py:41
  443.6 0.0 copy-start.4
  443.6 4.0 copy.20
  447.6 0.0 copy-done.4
  447.6 0.0 copy-start.3
  447.6 1.6 copy.19
  449.2 0.6 copy-done.3
  449.8 0.0 copy-start.5
  449.8 1.6 copy.18
  451.4 0.0 copy-done.5
  451.4 1.2 fusion.3
  452.7 0.0 copy-start.2
  452.7 4.5 fusion.5
  457.2 0.0 copy-done.2
  457.2 1.6 copy.17
  458.8 4.5 fusion.7
  463.3 0.0 copy-start.1
  463.3 9.5 %add_convert_fusion = bf16[64,128,256]{2,1,0:T(8,128)(2,1)} fusion(f32[64,128,256]{2,1,0:T(8,128)S(1)} %fusion.3, f32[64,128,256]{2,1,0:T(8,128)} %fusion.7, f32[64,128,256]{2,1,0:T(8,128)} %fusion.5, bf16[64,128,256]{2,1,0:T(8,128)(2,1)S(1)} %bitcast.60, bf16[4,1,256,256]{3,2,1,0:T(8,128)(2,1)} %param.6), kind=kOutput, calls=%fused_computation.1 | convolution fusion | flops 1082130432 | bytes 33685504 | tf_op jit(solution)/shard_map/src,cn->srn/dot_general | solution.py:39
  472.8 0.0 reduce-scatter.2.cloned.1.call-update
  472.8 53.5 %reduce-scatter.2.cloned.1.call-done = bf16[32,128,256]{2,1,0:T(8,128)(2,1)} async-done(((bf16[64,128,256]{2,1,0:T(8,128)(2,1)}), bf16[32,128,256]{2,1,0:T(8,128)(2,1)}) %reduce-scatter.2.cloned.1.call-update) | async-done | bytes 2097168 | tf_op jit(solution)/shard_map/reduce_scatter | solution.py:45
  526.3 0.0 copy-done.1
Async XLA Ops:
  6.5 20.0 %copy-start = (bf16[4,1,128,256]{3,2,1,0:T(8,128)(2,1)S(1)}, bf16[4,1,128,256]{3,2,1,0:T(8,128)(2,1)}, u32[]{:S(2)}) copy-start(bf16[4,1,128,256]{3,2,1,0:T(8,128)(2,1)} %param.5) | copy-start | bytes 786436
  6.5 4.2 copy-start.6
  6.5 20.0 %all-gather.2.cloned.1.call-start = ((), (), s32[]{:S(2)}) async-start(), calls=%async_computation.2 | async-start | bytes 6291456 | tf_op jit(solution)/shard_map/all_gather | solution.py:28
  10.7 515.6 %reduce-scatter.2.cloned.1.call-start = ((), (), s32[]{:S(2)}) async-start(), calls=%async_computation.3 | async-start | bytes 6291456 | tf_op jit(solution)/shard_map/reduce_scatter | solution.py:45
  443.6 4.0 copy-start.4
  447.6 2.2 copy-start.3
  449.8 1.6 copy-start.5
  452.7 4.5 copy-start.2
  463.3 63.0 %copy-start.1 = (bf16[4,1,128,256]{3,2,1,0:T(8,128)(2,1)S(1)}, bf16[4,1,128,256]{3,2,1,0:T(8,128)(2,1)}, u32[]{:S(2)}) copy-start(bf16[4,1,128,256]{3,2,1,0:T(8,128)(2,1)} %param.5) | copy-start | bytes 786436
Sparse Core Ops, SparseCore 0:
  10.8 15.6 all-gather.1
  472.9 53.3 reduce-scatter.1
where the time goes:
time: 534 us; the launch traced here: 533 us
  blocking collectives  368 us (69%)
  waiting for transfers between devices  69 us (13%)
  local copies, waits for them, and re-layouts  42.3 us (8%)
  matrix products  40.2 us (8%)
  between operations  13.5 us (3%)
    all_to_all x1, blocking collectives, shards(): lax.all_to_all(outgoing, 'block', split_axis=1, concat_axis=1, tiled=True)  368 us
    reduce_scatter x1, waiting for transfers between devices, shards(): lax.psum_scatter(partial_value.astype(jnp.bfloat16), 'term', scatter_dime...  53.5 us
    dot_general x4, matrix products, shards(): jnp.einsum('src,cn->srn', arrived[term_index], right_env[term_index, 0],...  19.7 us
    all_gather x1, waiting for transfers between devices, shards(): lax.all_gather(psi_blocks, 'half', axis=1, tiled=True)  15.4 us
    slice x5, local copies, waits for them, and re-layouts, shards(): arrived[term_index]  14.7 us
    convert_element_type x1, local copies, waits for them, and re-layouts, shards(): blended = jnp.einsum('wik,bkc->wbic', left_rows, lax.all_gather(psi_block...  14.6 us
    dot_general x1, matrix products, shards(): jnp.einsum('bs,wbrc->wsrc', dispatch, blended, preferred_element_type=jnp...  13.7 us
  transfers between devices with their start and end apart: 2, of which 2 were waited for; matrix products, arithmetic and copies ran while one was open for 0% of the time, Pallas kernels for 0%

commit v1 on v0

v1 whole, which is shorter than its diff:
```python
import functools

import jax
import jax.numpy as jnp
from jax import lax
from jax.experimental import pallas as pl
from jax.experimental.pallas import tpu as pltpu
from jax.sharding import PartitionSpec as P

MESH = pl.DeviceIdType.MESH
STEP = 1
AHEAD = 3


def slot_sources(right_owner, per_sector, n_block, capacity):
    source = lax.axis_index("block")
    targets = lax.dynamic_slice_in_dim(right_owner[:, 0], source * per_sector, per_sector)
    position = jnp.arange(per_sector, dtype=jnp.int32)
    upto = position[:, None] >= position[None, :]
    named = targets[None, :] == jnp.arange(n_block, dtype=jnp.int32)[:, None]
    count = jnp.sum((named[:, None, :] & upto[None]).astype(jnp.int32), axis=2)
    order = jnp.arange(capacity, dtype=jnp.int32)
    return jnp.sum((count[:, None, :] <= order[None, :, None]).astype(jnp.int32), axis=2).reshape(-1)


def kernel(
    n_block, capacity,
    idx, psi, left, right, out,
    stage, buf, lall, rall, mixed,
    z_send, z_recv, x_send, x_recv, s_send, s_recv,
    lz_send, lz_recv, lx_send, lx_recv, r_send, r_recv,
):
    z, x, h = lax.axis_index("block"), lax.axis_index("term"), lax.axis_index("half")
    per_sector, rows, width = psi.shape
    here = left.shape[0]
    terms = 2 * here
    share = capacity // 2
    steps = share // STEP
    per_core = here // 2
    owned = n_block // 2

    def remote(src, dst, send, recv, **where):
        return pltpu.make_async_remote_copy(
            src_ref=src, dst_ref=dst, send_sem=send, recv_sem=recv,
            device_id=where, device_id_type=MESH,
        )

    barrier = pltpu.get_barrier_semaphore()
    for d in range(1, n_block):
        pl.semaphore_signal(
            barrier, inc=1, device_id={"block": lax.rem(z + d, n_block)}, device_id_type=MESH)
    pl.semaphore_signal(barrier, inc=1, device_id={"term": 1 - x}, device_id_type=MESH)
    pl.semaphore_signal(barrier, inc=1, device_id={"half": 1 - h}, device_id_type=MESH)

    my_rows = pl.ds(pl.multiple_of(h * rows, rows), rows)
    other_rows = pl.ds(pl.multiple_of((1 - h) * rows, rows), rows)

    def slot(a, column, i, which):
        return buf.at[a, pl.ds(column * share + i * STEP, STEP), which, :]

    def l_part(a, column):
        return lall.at[a, pl.ds(column * here, here)]

    def l_up(a, src):
        return remote(src, l_part(a, x), lz_send.at[0, a], lz_recv.at[a], block=z + 1)

    def l_down(a, src):
        return remote(src, l_part(a, x), lz_send.at[1, a], lz_recv.at[a], block=z - 1)

    def l_cross(a, src):
        return remote(src, l_part(a, x), lx_send.at[lax.rem(a, owned)], lx_recv.at[lax.rem(a, owned)], term=1 - x)

    def l_cross_in(q):
        return remote(
            l_part(x * owned + q, 1 - x), l_part(x * owned + q, 1 - x), lx_send.at[q], lx_recv.at[q], term=1 - x)

    def pass_left(d):
        @pl.when(z - d >= 0)
        def _():
            a = z - d
            l_up(a, l_part(a, x)).wait_recv()

            @pl.when(z < n_block - 1)
            def _():
                l_up(a, l_part(a, x)).start()

            @pl.when(a // owned != x)
            def _():
                l_cross(a, l_part(a, x)).start()

        @pl.when(z + d < n_block)
        def _():
            a = z + d
            l_down(a, l_part(a, x)).wait_recv()

            @pl.when(z > 0)
            def _():
                l_down(a, l_part(a, x)).start()

            @pl.when(a // owned != x)
            def _():
                l_cross(a, l_part(a, x)).start()

    def r_part(column, core):
        return rall.at[pl.ds(column * here + core * per_core, per_core)]

    def r_cross():
        return remote(
            right.at[pl.ds(h * per_core, per_core)], r_part(x, h), r_send.at[0], r_recv.at[0], term=1 - x)

    def r_cross_in():
        return remote(r_part(1 - x, h), r_part(1 - x, h), r_send.at[0], r_recv.at[0], term=1 - x)

    def r_sibling():
        return remote(r_part(1 - x, h), r_part(1 - x, h), r_send.at[1], r_recv.at[1], half=1 - h)

    def r_sibling_in():
        return remote(r_part(1 - x, 1 - h), r_part(1 - x, 1 - h), r_send.at[1], r_recv.at[1], half=1 - h)

    def psi_out(d, i):
        b = lax.rem(z + d, n_block)
        return remote(
            stage.at[d - 1, pl.ds(i * STEP, STEP)], slot(z, x, i, my_rows),
            z_send.at[d - 1, i], z_recv.at[d - 1, i], block=b)

    def psi_in(d, i):
        a = lax.rem(z + n_block - d, n_block)
        return remote(
            stage.at[d - 1, pl.ds(i * STEP, STEP)], slot(a, x, i, my_rows),
            z_send.at[d - 1, i], z_recv.at[d - 1, i], block=a)

    def cross(a, i):
        q = lax.rem(a, owned)
        return remote(
            slot(a, x, i, my_rows), slot(a, x, i, my_rows), x_send.at[q, i], x_recv.at[q, i], term=1 - x)

    def cross_in(q, i):
        a = x * owned + q
        return remote(
            slot(a, 1 - x, i, my_rows), slot(a, 1 - x, i, my_rows), x_send.at[q, i], x_recv.at[q, i], term=1 - x)

    def sibling(q, column, i):
        a = x * owned + q
        return remote(
            slot(a, column, i, my_rows), slot(a, column, i, my_rows),
            s_send.at[q, column, i], s_recv.at[q, column, i], half=1 - h)

    def sibling_in(q, column, i):
        a = x * owned + q
        return remote(
            slot(a, column, i, other_rows), slot(a, column, i, other_rows),
            s_send.at[q, column, i], s_recv.at[q, column, i], half=1 - h)

    def block_for(b, i, s):
        j = idx[b * capacity + x * share + i * STEP + s]
        block = psi[jnp.minimum(j, per_sector - 1)]
        return jnp.where(j < per_sector, block, jnp.zeros_like(block))

    def send(i):
        for d in range(n_block - 1, 0, -1):
            b = lax.rem(z + d, n_block)
            for s in range(STEP):
                stage[d - 1, i * STEP + s] = block_for(b, i, s)
            psi_out(d, i).start()
        for s in range(STEP):
            buf[z, x * share + i * STEP + s, my_rows, :] = block_for(z, i, s)

    def hand_on(a, i):
        @pl.when(a // owned == x)
        def _():
            sibling(lax.rem(a, owned), x, i).start()

        @pl.when(a // owned != x)
        def _():
            cross(a, i).start()

    def product(i):
        count = owned * 2 * STEP

        def one(j, carry):
            q, rest = j // (2 * STEP), lax.rem(j, 2 * STEP)
            k = (rest // STEP) * share + i * STEP + lax.rem(rest, STEP)
            a = x * owned + q
            got = jnp.dot(
                lall[a].reshape(terms * rows, width), buf[a, k], preferred_element_type=jnp.float32)
            for w in range(terms):
                mixed[pl.ds(pl.multiple_of(j * rows, rows), rows), w * width:(w + 1) * width] = (
                    got[w * rows:(w + 1) * rows].astype(jnp.bfloat16))
            return carry

        lax.fori_loop(0, count, one, 0)
        span = here * width
        total = None
        for g in range(2):
            part = jnp.dot(
                mixed[:, g * span:(g + 1) * span], rall[g * here:(g + 1) * here].reshape(span, width),
                preferred_element_type=jnp.float32).astype(jnp.bfloat16).astype(jnp.float32)
            total = part if total is None else total + part
        total = total.astype(jnp.bfloat16)
        for q in range(owned):
            for c in range(2):
                for s in range(STEP):
                    j = (q * 2 + c) * STEP + s
                    out[q * capacity + c * share + i * STEP + s] = total[j * rows:(j + 1) * rows]

    pl.semaphore_wait(barrier, n_block + 1)

    @pl.when(z < n_block - 1)
    def _():
        l_up(z, left).start()

    @pl.when(z > 0)
    def _():
        l_down(z, left).start()

    @pl.when(z // owned != x)
    def _():
        l_cross(z, left).start()

    r_cross().start()
    for i in range(AHEAD):
        send(i)
    lall[z, pl.ds(x * here, here)] = left[...]
    rall[pl.ds(x * here, here)] = right[...]
    r_cross_in().wait_recv()
    r_sibling().start()

    def step(i, carry):
        for d in range(1, n_block):
            @pl.when(i == d - 1)
            def _():
                pass_left(d)

        @pl.when(i + AHEAD < steps)
        def _():
            send(i + AHEAD)

        @pl.when(i < steps)
        def _():
            hand_on(z, i)
            for d in range(1, n_block):
                psi_in(d, i).wait_recv()
                hand_on(lax.rem(z + n_block - d, n_block), i)

        @pl.when((i >= 1) & (i <= steps))
        def _():
            for q in range(owned):
                cross_in(q, i - 1).wait_recv()
                sibling(q, 1 - x, i - 1).start()

        @pl.when(i == 2)
        def _():
            r_sibling_in().wait_recv()
            for q in range(owned):
                l_cross_in(q).wait_recv()

        @pl.when(i >= 2)
        def _():
            for q in range(owned):
                for c in range(2):
                    sibling_in(q, c, i - 2).wait_recv()
            product(i - 2)

        return carry

    lax.fori_loop(0, steps + 2, step, 0)

    for a in range(n_block):
        @pl.when((z < n_block - 1) & (a <= z))
        def _():
            l_up(a, l_part(a, x)).wait_send()

        @pl.when((z > 0) & (a >= z))
        def _():
            l_down(a, l_part(a, x)).wait_send()
    for q in range(owned):
        l_cross((1 - x) * owned + q, l_part((1 - x) * owned + q, x)).wait_send()
    r_cross().wait_send()
    r_sibling().wait_send()

    def drain(i, carry):
        for d in range(1, n_block):
            psi_out(d, i).wait_send()
        for q in range(owned):
            cross((1 - x) * owned + q, i).wait_send()
            for c in range(2):
                sibling(q, c, i).wait_send()
        return carry

    lax.fori_loop(0, steps, drain, 0)


def owner_computes(psi_blocks, left_env, right_env, right_owner):
    n_block = lax.axis_size("block")
    per_sector, rows, width = psi_blocks.shape
    capacity = max(2, 2 * per_sector // n_block)
    here = left_env.shape[0]
    owned = n_block // 2
    share = capacity // 2
    steps = share // STEP
    idx = slot_sources(right_owner, per_sector, n_block, capacity)
    dma = pltpu.SemaphoreType.DMA
    vmem = pl.BlockSpec(memory_space=pltpu.VMEM)
    return pl.pallas_call(
        functools.partial(kernel, n_block, capacity),
        out_shape=jax.ShapeDtypeStruct((owned * capacity, rows, width), jnp.bfloat16),
        in_specs=[pl.BlockSpec(memory_space=pltpu.SMEM), vmem, vmem, vmem],
        out_specs=vmem,
        scratch_shapes=[
            pltpu.VMEM((n_block - 1, share, rows, width), jnp.bfloat16),
            pltpu.VMEM((n_block, capacity, 2 * rows, width), jnp.bfloat16),
            pltpu.VMEM((n_block, 2 * here, rows, width), jnp.bfloat16),
            pltpu.VMEM((2 * here, width, width), jnp.bfloat16),
            pltpu.VMEM((owned * 2 * STEP * rows, 2 * here * width), jnp.bfloat16),
            dma((n_block - 1, steps)), dma((n_block - 1, steps)),
            dma((owned, steps)), dma((owned, steps)),
            dma((owned, 2, steps)), dma((owned, 2, steps)),
            dma((2, n_block)), dma((n_block,)),
            dma((owned,)), dma((owned,)),
            dma((2,)), dma((2,)),
        ],
        compiler_params=pltpu.CompilerParams(
            collective_id=0, has_side_effects=True, vmem_limit_bytes=48 * 2**20),
    )(idx, psi_blocks, left_env[:, 0], right_env[:, 0])


def exchanged(psi_blocks, left_env, right_env, right_owner):
    n_block = lax.axis_size("block")
    per_sector = psi_blocks.shape[0]
    capacity = max(2, 2 * per_sector // n_block)
    rows, width = psi_blocks.shape[1], psi_blocks.shape[2]
    here = left_env.shape[0]
    idx = slot_sources(right_owner, per_sector, n_block, capacity)
    dispatch = (
        idx[:, None] == jnp.arange(per_sector, dtype=jnp.int32)[None, :]
    ).astype(jnp.bfloat16)
    blended = jnp.einsum(
        "wik,bkc->wbic", left_env[:, 0],
        lax.all_gather(psi_blocks, "half", axis=1, tiled=True),
        preferred_element_type=jnp.float32,
    ).astype(jnp.bfloat16)
    outgoing = jnp.einsum(
        "sb,wbrc->wsrc", dispatch, blended, preferred_element_type=jnp.float32
    ).astype(jnp.bfloat16)
    outgoing = outgoing.reshape(here, n_block, capacity, rows, width)
    arrived = lax.all_to_all(outgoing, "block", split_axis=1, concat_axis=1, tiled=True)
    arrived = arrived.reshape(here, n_block * capacity, rows, width)
    partial_value = jnp.zeros((n_block * capacity, rows, width), jnp.float32)
    for w in range(here):
        partial_value = partial_value + jnp.einsum(
            "src,cn->srn", arrived[w], right_env[w, 0], preferred_element_type=jnp.float32)
    return lax.psum_scatter(
        partial_value.astype(jnp.bfloat16), "term", scatter_dimension=0, tiled=True)


def solution(mesh):
    in_specs = (
        P(("groups", "block"), "half", None),
        P(("groups", "term"), "block", "half", None),
        P(("groups", "term"), "block", None, None),
        P("groups", None),
    )
    out_specs = P(("groups", "block", "term"), "half", None)
    small = mesh.shape["term"] == 2 and mesh.shape["half"] == 2 and mesh.shape["block"] == 4
    body = owner_computes if small else exchanged
    return jax.shard_map(body, mesh=mesh, in_specs=in_specs, out_specs=out_specs, check_vma=False)
```

time: 534 us -> 89 us (0.17)
  blocking collectives: 368 us -> 0 us
  Pallas kernels: 0 us -> 82.7 us
  waiting for transfers between devices: 69 us -> 0 us
  matrix products: 40.2 us -> 0 us
  local copies, waits for them, and re-layouts: 42.3 us -> 5.73 us
  between operations: 13.5 us -> 0.02 us
    all_to_all x1 -> x0, blocking collectives: 368 us -> none  [shards(): lax.all_to_all(outgoing, 'block', split_axis=1, concat_axis=1, tiled=True)]
    pallas_call x0 -> x1, Pallas kernels: none -> 82.7 us  [owner_computes(): pl.pallas_call(functools.partial(kernel, n_block, capacity), out_shape=ja...]
    reduce_scatter x1 -> x0, waiting for transfers between devices: 53.5 us -> none  [shards(): lax.psum_scatter(partial_value.astype(jnp.bfloat16), 'term', scatter_dime...]
    dot_general x6 -> x0, matrix products: 40.2 us -> none  [the longest x4 19.7 us: shards(): jnp.einsum('src,cn->srn', arrived[term_index], right_env[term_index, 0],...]
    all_gather x1 -> x0, waiting for transfers between devices: 15.4 us -> none  [shards(): lax.all_gather(psi_blocks, 'half', axis=1, tiled=True)]
    slice x5 -> x0, local copies, waits for them, and re-layouts: 14.7 us -> none  [shards(): arrived[term_index]]
    convert_element_type x1 -> x0, local copies, waits for them, and re-layouts: 14.6 us -> none  [shards(): blended = jnp.einsum('wik,bkc->wbic', left_rows, lax.all_gather(psi_block...]
    reshape x1, local copies, waits for them, and re-layouts: 8.18 us -> 0.09 us  [slot_sources(): jnp.sum((count[:, None, :] <= order[None, :, None]).astype(jnp.int32), ax...]
  transfers between devices with their start and end apart: 2 -> 0, of which waited for: 2 -> 0; matrix products, arithmetic and copies ran while one was open for 0% -> 0% of each run, Pallas kernels for 0% -> 0%
where the time goes in v1:
time: 89 us; the launch traced here: 88.7 us
  Pallas kernels  82.7 us (93%)
  local copies, waits for them, and re-layouts  5.73 us (6%)
    pallas_call x1, Pallas kernels, owner_computes(): pl.pallas_call(functools.partial(kernel, n_block, capacity), out_shape=ja...  82.7 us
    unnamed x9, local copies, waits for them, and re-layouts  5.57 us

profile of v1, /device:TPU:0, one launch (start us, length us, event | category | flops | bytes accessed | tf_op | source)
XLA Modules:
  0.0 88.7 jit_solution(4340216507188033845)
XLA Ops:
  0.0 0.0 copy-start
  0.0 0.7 copy-done
  0.7 0.1 dynamic-slice_bitcast_fusion
  0.7 0.1 convert_reduce_fusion
  0.9 0.1 convert_reduce_fusion.1
  1.0 0.1 reshape.38.idx
  1.1 0.0 copy-start.1
  1.1 1.6 %copy-done.1 = bf16[32,128,256]{2,1,0:T(8,128)(2,1)S(1)} copy-done((bf16[32,128,256]{2,1,0:T(8,128)(2,1)S(1)}, bf16[32,128,256]{2,1,0:T(8,128)(2,1)}, u32[]{:S(2)}) %copy-start.1) | copy-done | bytes 2097176
  2.7 0.0 copy-start.2
  2.7 1.0 %copy-done.2 = bf16[4,1,256,256]{3,2,1,0:T(8,128)(2,1)S(1)} copy-done((bf16[4,1,256,256]{3,2,1,0:T(8,128)(2,1)S(1)}, bf16[4,1,256,256]{3,2,1,0:T(8,128)(2,1)}, u32[]{:S(2)}) %copy-start.2) | copy-done | bytes 524312
  3.8 0.0 copy-start.3
  3.8 0.9 %copy-done.3 = bf16[4,1,128,256]{3,2,1,0:T(8,128)(2,1)S(1)} copy-done((bf16[4,1,128,256]{3,2,1,0:T(8,128)(2,1)S(1)}, bf16[4,1,128,256]{3,2,1,0:T(8,128)(2,1)}, u32[]{:S(2)}) %copy-start.3) | copy-done | bytes 262168
  4.7 82.7 %shard_map.46 = bf16[32,128,256]{2,1,0:T(8,128)(2,1)S(1)} custom-call(s32[64]{0:T(128)S(1)} %reshape.38.idx, bf16[32,128,256]{2,1,0:T(8,128)(2,1)S(1)} %copy-done.1, bf16[4,128,256]{2,1,0:T(8,128)(2,1)S(1)} %bitcast.5, bf16[4,256,256]{2,1,0:T(8,128)(2,1)S(1)} %bitcast.4), custom_call_target="tpu_custom_call" | custom-call | tf_op jit(solution)/shard_map/pallas_call | solution.py:304
  87.4 1.3 %copy.6 = bf16[32,128,256]{2,1,0:T(8,128)(2,1)} copy(bf16[32,128,256]{2,1,0:T(8,128)(2,1)S(1)} %shard_map.46) | data formatting | bytes 4194304
  (2 shorter events, 0.0 us)
Async XLA Ops:
  0.0 0.7 copy-start
  1.1 1.6 %copy-start.1 = (bf16[32,128,256]{2,1,0:T(8,128)(2,1)S(1)}, bf16[32,128,256]{2,1,0:T(8,128)(2,1)}, u32[]{:S(2)}) copy-start(bf16[32,128,256]{2,1,0:T(8,128)(2,1)} %psi.1) | copy-start | bytes 6291460
  2.7 1.0 %copy-start.2 = (bf16[4,1,256,256]{3,2,1,0:T(8,128)(2,1)S(1)}, bf16[4,1,256,256]{3,2,1,0:T(8,128)(2,1)}, u32[]{:S(2)}) copy-start(bf16[4,1,256,256]{3,2,1,0:T(8,128)(2,1)} %param.6) | copy-start | bytes 1572868
  3.8 0.9 %copy-start.3 = (bf16[4,1,128,256]{3,2,1,0:T(8,128)(2,1)S(1)}, bf16[4,1,128,256]{3,2,1,0:T(8,128)(2,1)}, u32[]{:S(2)}) copy-start(bf16[4,1,128,256]{3,2,1,0:T(8,128)(2,1)} %param.5) | copy-start | bytes 786436

commit v2 on v1

--- a/solution.py
+++ b/solution.py
@@ -9,7 +9,9 @@
 
 MESH = pl.DeviceIdType.MESH
 STEP = 1
-AHEAD = 3
+AHEAD = 4
+FIRST = 1
+LATE = 3
 
 
 def slot_sources(right_owner, per_sector, n_block, capacity):
@@ -26,9 +28,9 @@
 def kernel(
     n_block, capacity,
     idx, psi, left, right, out,
-    stage, buf, lall, rall, mixed,
+    psi_here, stage, buf, lall, rall, mixed, done,
     z_send, z_recv, x_send, x_recv, s_send, s_recv,
-    lz_send, lz_recv, lx_send, lx_recv, r_send, r_recv,
+    lz_send, lz_recv, lx_send, lx_recv, r_send, r_recv, own_sem, out_sem,
 ):
     z, x, h = lax.axis_index("block"), lax.axis_index("term"), lax.axis_index("half")
     per_sector, rows, width = psi.shape
@@ -45,6 +47,13 @@
             device_id=where, device_id_type=MESH,
         )
 
+    own = [
+        pltpu.make_async_copy(psi, psi_here, own_sem.at[0]),
+        pltpu.make_async_copy(left, lall.at[z, pl.ds(x * here, here)], own_sem.at[1]),
+        pltpu.make_async_copy(right, rall.at[pl.ds(x * here, here)], own_sem.at[2]),
+    ]
+    own[0].start()
+
     barrier = pltpu.get_barrier_semaphore()
     for d in range(1, n_block):
         pl.semaphore_signal(
@@ -153,7 +162,7 @@
 
     def block_for(b, i, s):
         j = idx[b * capacity + x * share + i * STEP + s]
-        block = psi[jnp.minimum(j, per_sector - 1)]
+        block = psi_here[jnp.minimum(j, per_sector - 1)]
         return jnp.where(j < per_sector, block, jnp.zeros_like(block))
 
     def send(i):
@@ -174,21 +183,26 @@
         def _():
             cross(a, i).start()
 
-    def product(i):
-        count = owned * 2 * STEP
+    def result(q, column, i):
+        at = pl.ds(q * capacity + column * share + i * STEP, STEP)
+        return pltpu.make_async_copy(done.at[at], out.at[at], out_sem.at[q, column, i])
+
+    def product(column, i):
+        first = column * share + i * STEP
+        for q in range(owned):
+            sibling_in(q, column, i).wait_recv()
 
         def one(j, carry):
-            q, rest = j // (2 * STEP), lax.rem(j, 2 * STEP)
-            k = (rest // STEP) * share + i * STEP + lax.rem(rest, STEP)
-            a = x * owned + q
+            q, s = j // STEP, lax.rem(j, STEP)
             got = jnp.dot(
-                lall[a].reshape(terms * rows, width), buf[a, k], preferred_element_type=jnp.float32)
+                lall[x * owned + q].reshape(terms * rows, width), buf[x * owned + q, first + s],
+                preferred_element_type=jnp.float32)
             for w in range(terms):
                 mixed[pl.ds(pl.multiple_of(j * rows, rows), rows), w * width:(w + 1) * width] = (
                     got[w * rows:(w + 1) * rows].astype(jnp.bfloat16))
             return carry
 
-        lax.fori_loop(0, count, one, 0)
+        lax.fori_loop(0, owned * STEP, one, 0)
         span = here * width
         total = None
         for g in range(2):
@@ -198,10 +212,21 @@
             total = part if total is None else total + part
         total = total.astype(jnp.bfloat16)
         for q in range(owned):
-            for c in range(2):
-                for s in range(STEP):
-                    j = (q * 2 + c) * STEP + s
-                    out[q * capacity + c * share + i * STEP + s] = total[j * rows:(j + 1) * rows]
+            for s in range(STEP):
+                j = q * STEP + s
+                done[q * capacity + first + s] = total[j * rows:(j + 1) * rows]
+            result(q, column, i).start()
+
+    def products(column, i, arrived):
+        def upto(t):
+            most = jnp.minimum(arrived + t - i, steps)
+            return jnp.where(t >= LATE, jnp.maximum(jnp.minimum(2 * (t - LATE) + 2, most), 0), 0)
+
+        def whole(n, carry):
+            product(column, n)
+            return carry
+
+        lax.fori_loop(upto(i - 1), upto(i), whole, 0)
 
     pl.semaphore_wait(barrier, n_block + 1)
 
@@ -218,19 +243,22 @@
         l_cross(z, left).start()
 
     r_cross().start()
-    for i in range(AHEAD):
+    own[0].wait()
+    own[1].start()
+    own[2].start()
+    for i in range(FIRST):
         send(i)
-    lall[z, pl.ds(x * here, here)] = left[...]
-    rall[pl.ds(x * here, here)] = right[...]
     r_cross_in().wait_recv()
     r_sibling().start()
 
+    for d in range(1, n_block):
+        pass_left(d)
+        if FIRST + d <= AHEAD:
+            send(FIRST + d - 1)
+    for i in range(FIRST + n_block - 1, AHEAD):
+        send(i)
+
     def step(i, carry):
-        for d in range(1, n_block):
-            @pl.when(i == d - 1)
-            def _():
-                pass_left(d)
-
         @pl.when(i + AHEAD < steps)
         def _():
             send(i + AHEAD)
@@ -242,25 +270,23 @@
                 psi_in(d, i).wait_recv()
                 hand_on(lax.rem(z + n_block - d, n_block), i)
 
+        @pl.when(i == LATE)
+        def _():
+            own[1].wait()
+            own[2].wait()
+            r_sibling_in().wait_recv()
+            for q in range(owned):
+                l_cross_in(q).wait_recv()
+
+        products(x, i, i)
+
         @pl.when((i >= 1) & (i <= steps))
         def _():
             for q in range(owned):
                 cross_in(q, i - 1).wait_recv()
                 sibling(q, 1 - x, i - 1).start()
 
-        @pl.when(i == 2)
-        def _():
-            r_sibling_in().wait_recv()
-            for q in range(owned):
-                l_cross_in(q).wait_recv()
-
-        @pl.when(i >= 2)
-        def _():
-            for q in range(owned):
-                for c in range(2):
-                    sibling_in(q, c, i - 2).wait_recv()
-            product(i - 2)
-
+        products(1 - x, i, i - 1)
         return carry
 
     lax.fori_loop(0, steps + 2, step, 0)
@@ -285,6 +311,7 @@
             cross((1 - x) * owned + q, i).wait_send()
             for c in range(2):
                 sibling(q, c, i).wait_send()
+                result(q, c, i).wait()
         return carry
 
     lax.fori_loop(0, steps, drain, 0)
@@ -300,27 +327,30 @@
     steps = share // STEP
     idx = slot_sources(right_owner, per_sector, n_block, capacity)
     dma = pltpu.SemaphoreType.DMA
-    vmem = pl.BlockSpec(memory_space=pltpu.VMEM)
+    anywhere = pl.BlockSpec(memory_space=pl.ANY)
     return pl.pallas_call(
         functools.partial(kernel, n_block, capacity),
         out_shape=jax.ShapeDtypeStruct((owned * capacity, rows, width), jnp.bfloat16),
-        in_specs=[pl.BlockSpec(memory_space=pltpu.SMEM), vmem, vmem, vmem],
-        out_specs=vmem,
+        in_specs=[pl.BlockSpec(memory_space=pltpu.SMEM), anywhere, anywhere, anywhere],
+        out_specs=anywhere,
         scratch_shapes=[
+            pltpu.VMEM((per_sector, rows, width), jnp.bfloat16),
             pltpu.VMEM((n_block - 1, share, rows, width), jnp.bfloat16),
             pltpu.VMEM((n_block, capacity, 2 * rows, width), jnp.bfloat16),
             pltpu.VMEM((n_block, 2 * here, rows, width), jnp.bfloat16),
             pltpu.VMEM((2 * here, width, width), jnp.bfloat16),
-            pltpu.VMEM((owned * 2 * STEP * rows, 2 * here * width), jnp.bfloat16),
+            pltpu.VMEM((owned * STEP * rows, 2 * here * width), jnp.bfloat16),
+            pltpu.VMEM((owned * capacity, rows, width), jnp.bfloat16),
             dma((n_block - 1, steps)), dma((n_block - 1, steps)),
             dma((owned, steps)), dma((owned, steps)),
             dma((owned, 2, steps)), dma((owned, 2, steps)),
             dma((2, n_block)), dma((n_block,)),
             dma((owned,)), dma((owned,)),
             dma((2,)), dma((2,)),
+            dma((3,)), dma((owned, 2, steps)),
         ],
         compiler_params=pltpu.CompilerParams(
-            collective_id=0, has_side_effects=True, vmem_limit_bytes=48 * 2**20),
+            collective_id=0, has_side_effects=True, vmem_limit_bytes=60 * 2**20),
     )(idx, psi_blocks, left_env[:, 0], right_env[:, 0])
 
 

time: 89 us -> 79.7 us (0.90)
  Pallas kernels: 82.7 us -> 74.8 us
  local copies, waits for them, and re-layouts: 5.73 us -> 4.46 us
    pallas_call x1, Pallas kernels: 82.7 us -> 74.8 us  [owner_computes(): pl.pallas_call(functools.partial(kernel, n_block, capacity), out_shape=ja...]
    unnamed x9 -> x3, local copies, waits for them, and re-layouts: 5.57 us -> 3.78 us
where the time goes in v2:
time: 79.7 us; the launch traced here: 79.6 us
  Pallas kernels  74.8 us (94%)
  local copies, waits for them, and re-layouts  4.46 us (6%)
    pallas_call x1, Pallas kernels, owner_computes(): pl.pallas_call(functools.partial(kernel, n_block, capacity), out_shape=ja...  74.8 us
    unnamed x3, local copies, waits for them, and re-layouts  3.78 us

profile of v2, /device:TPU:0, one launch (start us, length us, event | category | flops | bytes accessed | tf_op | source)
XLA Modules:
  0.0 79.6 jit_solution(7784073568092705888)
XLA Ops:
  0.0 0.0 copy-start
  0.0 0.7 copy-done
  0.7 0.1 dynamic-slice_bitcast_fusion
  0.7 0.1 convert_reduce_fusion
  0.9 0.1 convert_reduce_fusion.1
  1.0 0.6 reshape.38.idx
  1.7 74.8 %shard_map.46 = bf16[32,128,256]{2,1,0:T(8,128)(2,1)} custom-call(s32[64]{0:T(128)} %reshape.38.idx, bf16[32,128,256]{2,1,0:T(8,128)(2,1)} %psi.1, bf16[4,128,256]{2,1,0:T(8,128)(2,1)} %bitcast.5, bf16[4,256,256]{2,1,0:T(8,128)(2,1)} %bitcast.4), custom_call_target="tpu_custom_call" | custom-call | tf_op jit(solution)/shard_map/pallas_call | solution.py:331
  76.4 3.1 %copy.6 = bf16[32,128,256]{2,1,0:T(8,128)(2,1)} copy(bf16[32,128,256]{2,1,0:T(8,128)(2,1)} %shard_map.46) | data formatting | bytes 4194304
  (2 shorter events, 0.0 us)
Async XLA Ops:
  0.0 0.7 copy-start

commit v3 on v2

--- a/solution.py
+++ b/solution.py
@@ -9,8 +9,9 @@
 
 MESH = pl.DeviceIdType.MESH
 STEP = 1
-AHEAD = 4
+AHEAD = 5
 FIRST = 1
+PIECES = 4
 LATE = 3
 
 
@@ -28,9 +29,9 @@
 def kernel(
     n_block, capacity,
     idx, psi, left, right, out,
-    psi_here, stage, buf, lall, rall, mixed, done,
+    psi_here, stage, buf, lall, rall, mixed,
     z_send, z_recv, x_send, x_recv, s_send, s_recv,
-    lz_send, lz_recv, lx_send, lx_recv, r_send, r_recv, own_sem, out_sem,
+    lz_send, lz_recv, lx_send, lx_recv, r_send, r_recv, own_sem,
 ):
     z, x, h = lax.axis_index("block"), lax.axis_index("term"), lax.axis_index("half")
     per_sector, rows, width = psi.shape
@@ -67,48 +68,55 @@
     def slot(a, column, i, which):
         return buf.at[a, pl.ds(column * share + i * STEP, STEP), which, :]
 
-    def l_part(a, column):
-        return lall.at[a, pl.ds(column * here, here)]
-
-    def l_up(a, src):
-        return remote(src, l_part(a, x), lz_send.at[0, a], lz_recv.at[a], block=z + 1)
-
-    def l_down(a, src):
-        return remote(src, l_part(a, x), lz_send.at[1, a], lz_recv.at[a], block=z - 1)
-
-    def l_cross(a, src):
-        return remote(src, l_part(a, x), lx_send.at[lax.rem(a, owned)], lx_recv.at[lax.rem(a, owned)], term=1 - x)
-
-    def l_cross_in(q):
-        return remote(
-            l_part(x * owned + q, 1 - x), l_part(x * owned + q, 1 - x), lx_send.at[q], lx_recv.at[q], term=1 - x)
-
-    def pass_left(d):
+    part = here // PIECES
+
+    def l_part(a, column, p):
+        return lall.at[a, pl.ds(column * here + p * part, part)]
+
+    def l_own(p):
+        return left.at[pl.ds(p * part, part)]
+
+    def l_up(a, p, src):
+        return remote(src, l_part(a, x, p), lz_send.at[0, a, p], lz_recv.at[a, p], block=z + 1)
+
+    def l_down(a, p, src):
+        return remote(src, l_part(a, x, p), lz_send.at[1, a, p], lz_recv.at[a, p], block=z - 1)
+
+    def l_cross(a, p, src):
+        q = lax.rem(a, owned)
+        return remote(src, l_part(a, x, p), lx_send.at[q, p], lx_recv.at[q, p], term=1 - x)
+
+    def l_cross_in(q, p):
+        a = x * owned + q
+        return remote(
+            l_part(a, 1 - x, p), l_part(a, 1 - x, p), lx_send.at[q, p], lx_recv.at[q, p], term=1 - x)
+
+    def pass_left(d, p):
         @pl.when(z - d >= 0)
         def _():
             a = z - d
-            l_up(a, l_part(a, x)).wait_recv()
+            l_up(a, p, l_part(a, x, p)).wait_recv()
 
             @pl.when(z < n_block - 1)
             def _():
-                l_up(a, l_part(a, x)).start()
+                l_up(a, p, l_part(a, x, p)).start()
 
             @pl.when(a // owned != x)
             def _():
-                l_cross(a, l_part(a, x)).start()
+                l_cross(a, p, l_part(a, x, p)).start()
 
         @pl.when(z + d < n_block)
         def _():
             a = z + d
-            l_down(a, l_part(a, x)).wait_recv()
+            l_down(a, p, l_part(a, x, p)).wait_recv()
 
             @pl.when(z > 0)
             def _():
-                l_down(a, l_part(a, x)).start()
+                l_down(a, p, l_part(a, x, p)).start()
 
             @pl.when(a // owned != x)
             def _():
-                l_cross(a, l_part(a, x)).start()
+                l_cross(a, p, l_part(a, x, p)).start()
 
     def r_part(column, core):
         return rall.at[pl.ds(column * here + core * per_core, per_core)]
@@ -166,7 +174,7 @@
         return jnp.where(j < per_sector, block, jnp.zeros_like(block))
 
     def send(i):
-        for d in range(n_block - 1, 0, -1):
+        for d in range(1, n_block):
             b = lax.rem(z + d, n_block)
             for s in range(STEP):
                 stage[d - 1, i * STEP + s] = block_for(b, i, s)
@@ -182,10 +190,6 @@
         @pl.when(a // owned != x)
         def _():
             cross(a, i).start()
-
-    def result(q, column, i):
-        at = pl.ds(q * capacity + column * share + i * STEP, STEP)
-        return pltpu.make_async_copy(done.at[at], out.at[at], out_sem.at[q, column, i])
 
     def product(column, i):
         first = column * share + i * STEP
@@ -214,8 +218,7 @@
         for q in range(owned):
             for s in range(STEP):
                 j = q * STEP + s
-                done[q * capacity + first + s] = total[j * rows:(j + 1) * rows]
-            result(q, column, i).start()
+                out[q * capacity + first + s] = total[j * rows:(j + 1) * rows]
 
     def products(column, i, arrived):
         def upto(t):
@@ -230,17 +233,18 @@
 
     pl.semaphore_wait(barrier, n_block + 1)
 
-    @pl.when(z < n_block - 1)
-    def _():
-        l_up(z, left).start()
-
-    @pl.when(z > 0)
-    def _():
-        l_down(z, left).start()
-
-    @pl.when(z // owned != x)
-    def _():
-        l_cross(z, left).start()
+    for p in range(PIECES):
+        @pl.when(z < n_block - 1)
+        def _():
+            l_up(z, p, l_own(p)).start()
+
+        @pl.when(z > 0)
+        def _():
+            l_down(z, p, l_own(p)).start()
+
+        @pl.when(z // owned != x)
+        def _():
+            l_cross(z, p, l_own(p)).start()
 
     r_cross().start()
     own[0].wait()
@@ -252,7 +256,8 @@
     r_sibling().start()
 
     for d in range(1, n_block):
-        pass_left(d)
+        for p in range(PIECES):
+            pass_left(d, p)
         if FIRST + d <= AHEAD:
             send(FIRST + d - 1)
     for i in range(FIRST + n_block - 1, AHEAD):
@@ -276,7 +281,8 @@
             own[2].wait()
             r_sibling_in().wait_recv()
             for q in range(owned):
-                l_cross_in(q).wait_recv()
+                for p in range(PIECES):
+                    l_cross_in(q, p).wait_recv()
 
         products(x, i, i)
 
@@ -291,16 +297,18 @@
 
     lax.fori_loop(0, steps + 2, step, 0)
 
-    for a in range(n_block):
-        @pl.when((z < n_block - 1) & (a <= z))
-        def _():
-            l_up(a, l_part(a, x)).wait_send()
-
-        @pl.when((z > 0) & (a >= z))
-        def _():
-            l_down(a, l_part(a, x)).wait_send()
-    for q in range(owned):
-        l_cross((1 - x) * owned + q, l_part((1 - x) * owned + q, x)).wait_send()
+    for p in range(PIECES):
+        for a in range(n_block):
+            @pl.when((z < n_block - 1) & (a <= z))
+            def _():
+                l_up(a, p, l_part(a, x, p)).wait_send()
+
+            @pl.when((z > 0) & (a >= z))
+            def _():
+                l_down(a, p, l_part(a, x, p)).wait_send()
+        for q in range(owned):
+            a = (1 - x) * owned + q
+            l_cross(a, p, l_part(a, x, p)).wait_send()
     r_cross().wait_send()
     r_sibling().wait_send()
 
@@ -311,7 +319,6 @@
             cross((1 - x) * owned + q, i).wait_send()
             for c in range(2):
                 sibling(q, c, i).wait_send()
-                result(q, c, i).wait()
         return carry
 
     lax.fori_loop(0, steps, drain, 0)
@@ -327,12 +334,12 @@
     steps = share // STEP
     idx = slot_sources(right_owner, per_sector, n_block, capacity)
     dma = pltpu.SemaphoreType.DMA
-    anywhere = pl.BlockSpec(memory_space=pl.ANY)
+    hbm = pl.BlockSpec(memory_space=pltpu.HBM)
     return pl.pallas_call(
         functools.partial(kernel, n_block, capacity),
         out_shape=jax.ShapeDtypeStruct((owned * capacity, rows, width), jnp.bfloat16),
-        in_specs=[pl.BlockSpec(memory_space=pltpu.SMEM), anywhere, anywhere, anywhere],
-        out_specs=anywhere,
+        in_specs=[pl.BlockSpec(memory_space=pltpu.SMEM), hbm, hbm, hbm],
+        out_specs=pl.BlockSpec(memory_space=pltpu.VMEM),
         scratch_shapes=[
             pltpu.VMEM((per_sector, rows, width), jnp.bfloat16),
             pltpu.VMEM((n_block - 1, share, rows, width), jnp.bfloat16),
@@ -340,17 +347,16 @@
             pltpu.VMEM((n_block, 2 * here, rows, width), jnp.bfloat16),
             pltpu.VMEM((2 * here, width, width), jnp.bfloat16),
             pltpu.VMEM((owned * STEP * rows, 2 * here * width), jnp.bfloat16),
-            pltpu.VMEM((owned * capacity, rows, width), jnp.bfloat16),
             dma((n_block - 1, steps)), dma((n_block - 1, steps)),
             dma((owned, steps)), dma((owned, steps)),
             dma((owned, 2, steps)), dma((owned, 2, steps)),
-            dma((2, n_block)), dma((n_block,)),
-            dma((owned,)), dma((owned,)),
+            dma((2, n_block, PIECES)), dma((n_block, PIECES)),
+            dma((owned, PIECES)), dma((owned, PIECES)),
             dma((2,)), dma((2,)),
-            dma((3,)), dma((owned, 2, steps)),
+            dma((3,)),
         ],
         compiler_params=pltpu.CompilerParams(
-            collective_id=0, has_side_effects=True, vmem_limit_bytes=60 * 2**20),
+            collective_id=0, has_side_effects=True, vmem_limit_bytes=36 * 2**20),
     )(idx, psi_blocks, left_env[:, 0], right_env[:, 0])
 
 

time: 79.7 us -> 77.9 us (0.977)
  Pallas kernels: 74.8 us -> 71.7 us
  local copies, waits for them, and re-layouts: 4.46 us -> 5.73 us
    pallas_call x1, Pallas kernels: 74.8 us -> 71.7 us  [owner_computes(): pl.pallas_call(functools.partial(kernel, n_block, capacity), out_shape=ja...]
    unnamed x3 -> x9, local copies, waits for them, and re-layouts: 3.78 us -> 5.57 us
where the time goes in v3:
time: 77.9 us; the launch traced here: 77.7 us
  Pallas kernels  71.7 us (92%)
  local copies, waits for them, and re-layouts  5.73 us (7%)
    pallas_call x1, Pallas kernels, owner_computes(): pl.pallas_call(functools.partial(kernel, n_block, capacity), out_shape=ja...  71.7 us
    unnamed x9, local copies, waits for them, and re-layouts  5.57 us

profile of v3, /device:TPU:0, one launch (start us, length us, event | category | flops | bytes accessed | tf_op | source)
XLA Modules:
  0.0 77.7 jit_solution(16485229705033092722)
XLA Ops:
  0.0 0.0 copy-start
  0.0 0.7 copy-done
  0.7 0.1 dynamic-slice_bitcast_fusion
  0.7 0.1 convert_reduce_fusion
  0.9 0.1 convert_reduce_fusion.1
  1.0 0.1 reshape.38.idx
  1.1 0.0 copy-start.1
  1.1 1.6 %copy-done.1 = bf16[32,128,256]{2,1,0:T(8,128)(2,1)S(1)} copy-done((bf16[32,128,256]{2,1,0:T(8,128)(2,1)S(1)}, bf16[32,128,256]{2,1,0:T(8,128)(2,1)}, u32[]{:S(2)}) %copy-start.1) | copy-done | bytes 2097176
  2.7 0.0 copy-start.2
  2.7 1.0 %copy-done.2 = bf16[4,1,256,256]{3,2,1,0:T(8,128)(2,1)S(1)} copy-done((bf16[4,1,256,256]{3,2,1,0:T(8,128)(2,1)S(1)}, bf16[4,1,256,256]{3,2,1,0:T(8,128)(2,1)}, u32[]{:S(2)}) %copy-start.2) | copy-done | bytes 524312
  3.8 0.0 copy-start.3
  3.8 0.9 %copy-done.3 = bf16[4,1,128,256]{3,2,1,0:T(8,128)(2,1)S(1)} copy-done((bf16[4,1,128,256]{3,2,1,0:T(8,128)(2,1)S(1)}, bf16[4,1,128,256]{3,2,1,0:T(8,128)(2,1)}, u32[]{:S(2)}) %copy-start.3) | copy-done | bytes 262168
  4.7 71.7 %shard_map.46 = bf16[32,128,256]{2,1,0:T(8,128)(2,1)S(1)} custom-call(s32[64]{0:T(128)S(1)} %reshape.38.idx, bf16[32,128,256]{2,1,0:T(8,128)(2,1)S(1)} %copy-done.1, bf16[4,128,256]{2,1,0:T(8,128)(2,1)S(1)} %bitcast.5, bf16[4,256,256]{2,1,0:T(8,128)(2,1)S(1)} %bitcast.4), custom_call_target="tpu_custom_call" | custom-call | tf_op jit(solution)/shard_map/pallas_call | solution.py:338
  76.4 1.3 %copy.6 = bf16[32,128,256]{2,1,0:T(8,128)(2,1)} copy(bf16[32,128,256]{2,1,0:T(8,128)(2,1)S(1)} %shard_map.46) | data formatting | bytes 4194304
  (2 shorter events, 0.0 us)
Async XLA Ops:
  0.0 0.7 copy-start
  1.1 1.6 %copy-start.1 = (bf16[32,128,256]{2,1,0:T(8,128)(2,1)S(1)}, bf16[32,128,256]{2,1,0:T(8,128)(2,1)}, u32[]{:S(2)}) copy-start(bf16[32,128,256]{2,1,0:T(8,128)(2,1)} %psi.1) | copy-start | bytes 6291460
  2.7 1.0 %copy-start.2 = (bf16[4,1,256,256]{3,2,1,0:T(8,128)(2,1)S(1)}, bf16[4,1,256,256]{3,2,1,0:T(8,128)(2,1)}, u32[]{:S(2)}) copy-start(bf16[4,1,256,256]{3,2,1,0:T(8,128)(2,1)} %param.6) | copy-start | bytes 1572868
  3.8 0.9 %copy-start.3 = (bf16[4,1,128,256]{3,2,1,0:T(8,128)(2,1)S(1)}, bf16[4,1,128,256]{3,2,1,0:T(8,128)(2,1)}, u32[]{:S(2)}) copy-start(bf16[4,1,128,256]{3,2,1,0:T(8,128)(2,1)} %param.5) | copy-start | bytes 786436

commit v4 on v3

--- a/solution.py
+++ b/solution.py
@@ -256,11 +256,11 @@
     r_sibling().start()
 
     for d in range(1, n_block):
+        if FIRST + d <= AHEAD and d > 1:
+            send(FIRST + d - 2)
         for p in range(PIECES):
             pass_left(d, p)
-        if FIRST + d <= AHEAD:
-            send(FIRST + d - 1)
-    for i in range(FIRST + n_block - 1, AHEAD):
+    for i in range(FIRST + n_block - 2, AHEAD):
         send(i)
 
     def step(i, carry):

time: 77.9 us -> 77.9 us (level)
  no operation moved by 1% of the time
where the time goes in v4:
time: 77.9 us; the launch traced here: 77.7 us
  Pallas kernels  71.7 us (92%)
  local copies, waits for them, and re-layouts  5.73 us (7%)
    pallas_call x1, Pallas kernels, owner_computes(): pl.pallas_call(functools.partial(kernel, n_block, capacity), out_shape=ja...  71.7 us
    unnamed x9, local copies, waits for them, and re-layouts  5.57 us

profile of v4, /device:TPU:0, one launch (start us, length us, event | category | flops | bytes accessed | tf_op | source)
XLA Modules:
  0.0 77.7 jit_solution(16485229705033092722)
XLA Ops:
  0.0 0.0 copy-start
  0.0 0.7 copy-done
  0.7 0.1 dynamic-slice_bitcast_fusion
  0.7 0.1 convert_reduce_fusion
  0.9 0.1 convert_reduce_fusion.1
  1.0 0.1 reshape.38.idx
  1.1 0.0 copy-start.1
  1.1 1.6 %copy-done.1 = bf16[32,128,256]{2,1,0:T(8,128)(2,1)S(1)} copy-done((bf16[32,128,256]{2,1,0:T(8,128)(2,1)S(1)}, bf16[32,128,256]{2,1,0:T(8,128)(2,1)}, u32[]{:S(2)}) %copy-start.1) | copy-done | bytes 2097176
  2.7 0.0 copy-start.2
  2.7 1.0 %copy-done.2 = bf16[4,1,256,256]{3,2,1,0:T(8,128)(2,1)S(1)} copy-done((bf16[4,1,256,256]{3,2,1,0:T(8,128)(2,1)S(1)}, bf16[4,1,256,256]{3,2,1,0:T(8,128)(2,1)}, u32[]{:S(2)}) %copy-start.2) | copy-done | bytes 524312
  3.8 0.0 copy-start.3
  3.8 0.9 %copy-done.3 = bf16[4,1,128,256]{3,2,1,0:T(8,128)(2,1)S(1)} copy-done((bf16[4,1,128,256]{3,2,1,0:T(8,128)(2,1)S(1)}, bf16[4,1,128,256]{3,2,1,0:T(8,128)(2,1)}, u32[]{:S(2)}) %copy-start.3) | copy-done | bytes 262168
  4.7 71.7 %shard_map.46 = bf16[32,128,256]{2,1,0:T(8,128)(2,1)S(1)} custom-call(s32[64]{0:T(128)S(1)} %reshape.38.idx, bf16[32,128,256]{2,1,0:T(8,128)(2,1)S(1)} %copy-done.1, bf16[4,128,256]{2,1,0:T(8,128)(2,1)S(1)} %bitcast.5, bf16[4,256,256]{2,1,0:T(8,128)(2,1)S(1)} %bitcast.4), custom_call_target="tpu_custom_call" | custom-call | tf_op jit(solution)/shard_map/pallas_call | solution.py:338
  76.4 1.3 %copy.6 = bf16[32,128,256]{2,1,0:T(8,128)(2,1)} copy(bf16[32,128,256]{2,1,0:T(8,128)(2,1)S(1)} %shard_map.46) | data formatting | bytes 4194304
  (2 shorter events, 0.0 us)
Async XLA Ops:
  0.0 0.7 copy-start
  1.1 1.6 %copy-start.1 = (bf16[32,128,256]{2,1,0:T(8,128)(2,1)S(1)}, bf16[32,128,256]{2,1,0:T(8,128)(2,1)}, u32[]{:S(2)}) copy-start(bf16[32,128,256]{2,1,0:T(8,128)(2,1)} %psi.1) | copy-start | bytes 6291460
  2.7 1.0 %copy-start.2 = (bf16[4,1,256,256]{3,2,1,0:T(8,128)(2,1)S(1)}, bf16[4,1,256,256]{3,2,1,0:T(8,128)(2,1)}, u32[]{:S(2)}) copy-start(bf16[4,1,256,256]{3,2,1,0:T(8,128)(2,1)} %param.6) | copy-start | bytes 1572868
  3.8 0.9 %copy-start.3 = (bf16[4,1,128,256]{3,2,1,0:T(8,128)(2,1)S(1)}, bf16[4,1,128,256]{3,2,1,0:T(8,128)(2,1)}, u32[]{:S(2)}) copy-start(bf16[4,1,128,256]{3,2,1,0:T(8,128)(2,1)} %param.5) | copy-start | bytes 786436
